TPU v7x, 32 devices: a whole 2x2x4 slice. The times are simulated.
32 devices in a mesh: ctx: 2 (over x), tp: 4 (over z), dp: 4 (over y, core).
Axes of the slice: x: 2, y: 2, z: 4, core: 2. Of those that a mesh axis runs over, the one named last changes fastest.
Arguments:
- trailing_questions: bfloat16 [1024, 8192], P(('dp', 'ctx'), 'tp'), parts along dimension 0, may hold values from -6 to 6
- output_gradient: bfloat16 [1024, 8192], P(('dp', 'ctx'), 'tp'), parts along dimension 0, may hold values from -6 to 6
- tail_row_key: bfloat16 [1024, 1024], P(('dp', 'ctx'), 'tp'), parts along dimension 0, may hold values from -6 to 6
- tail_row_value: bfloat16 [1024, 1024], P(('dp', 'ctx'), 'tp'), parts along dimension 0, may hold values from -6 to 6
- passage_key_cache: bfloat16 [2048, 1024], P(('dp', 'ctx'), 'tp'), parts along dimension 0, may hold values from -6 to 6
- passage_value_cache: bfloat16 [2048, 1024], P(('dp', 'ctx'), 'tp'), parts along dimension 0, may hold values from -6 to 6
- row_list: int32 [1024], P(('dp', 'ctx')), parts along dimension 0, may hold values from 0 to 1, as said below
- read_owner: int32 [8, 24], P(('dp', 'ctx')), parts along dimension 0, may hold values from 0 to 1, as said below
- read_tile: int32 [8, 24], P(('dp', 'ctx')), parts along dimension 0, may hold values from 0 to 1
- read_list: int32 [8, 24], P(('dp', 'ctx')), parts along dimension 0, may hold values from 0 to 1
- read_count: int32 [8], P(('dp', 'ctx')), parts along dimension 0, may hold values from 12 to 24, as said below
Outputs:
- grad_query: bfloat16 [1024, 8192], P(('dp', 'ctx'), 'tp'), parts along dimension 0
- grad_tail_key: bfloat16 [1024, 1024], P(('dp', 'ctx'), 'tp'), parts along dimension 0
- grad_tail_value: bfloat16 [1024, 1024], P(('dp', 'ctx'), 'tp'), parts along dimension 0
- grad_key_cache: float32 [2048, 1024], P(('dp', 'ctx'), 'tp'), parts along dimension 0
- grad_value_cache: float32 [2048, 1024], P(('dp', 'ctx'), 'tp'), parts along dimension 0
There are 4 independent parts, one for each index of `dp`. A program takes and returns all parts, laid end to end along the dimension named above; each array names one. Nothing has to cross between parts.
Inputs may be any that keep to these rules, and one draw needn't show every extreme that they name: `row_list`: on each reader's 128 rows the list number is 0 on a first run and 1 on the rest; both runs are nonempty. `read_owner`: a reader names one owner at most 12 times, and every reader names some owner exactly 12 times. `read_count`: some reader has all 24 reads live.
All inputs are finite; a program needn't handle non-finite values.
Results may differ from a plain program's by a relative error of at most 0.012.
Values may be sent and summed in bfloat16 or wider, within the bound.
No kernel may reach another device: no remote copies, remote signals or barrier semaphores. Data moves between devices by JAX's collectives and lax.ppermute only.
A program may use at most 64 MiB of HBM per device.

v0:
```python
import functools
import math

import jax
import jax.numpy as jnp
from jax import lax
from jax.experimental import pallas as pl
from jax.experimental.pallas import tpu as pltpu
from jax.sharding import PartitionSpec as P

WIDTH = 128
TILE = 128
PAIR = 2 * WIDTH
NEAR_OUTS = 8
NEG = -1e30
SCALE = 1.0 / math.sqrt(WIDTH)
SCALE2 = SCALE * math.log2(math.e)
F32 = jnp.float32
BF16 = jnp.bfloat16


def dot_nt(a, b):
    return lax.dot_general(a, b, (((1,), (1,)), ((), ())), preferred_element_type=F32)


def dot_nn(a, b):
    return lax.dot_general(a, b, (((1,), (0,)), ((), ())), preferred_element_type=F32)


def dot_tn(a, b):
    return lax.dot_general(a, b, (((0,), (0,)), ((), ())), preferred_element_type=F32)


def repeat(steps, unroll, step):
    if unroll:
        for i in range(steps):
            step(i)
    else:

        def one(i, carry):
            step(i)
            return carry

        lax.fori_loop(0, steps, one, 0)


def added(steps, unroll, step, total_ref):
    if unroll:
        return functools.reduce(jnp.add, [step(i) for i in range(steps)])
    (total_ref,) = total_ref
    total_ref[...] = jnp.zeros_like(total_ref)

    def one(i):
        total_ref[...] += step(i)

    repeat(steps, unroll, one)
    return total_ref[...]


def columns(i, width):
    if isinstance(i, int):
        return pl.ds(i * width, width)
    return pl.ds(pl.multiple_of(i * width, width), width)


def pair_rows(ref, i):
    block = ref[:, columns(i, PAIR)]
    return jnp.concatenate([block[:, :WIDTH], block[:, WIDTH:]], axis=0)


def stacked_rows(ref, head, group):
    first = head * group
    return jnp.concatenate(
        [ref[:, (first + g) * WIDTH : (first + g + 1) * WIDTH] for g in range(group)], axis=0
    )


def twice(row):
    return jnp.concatenate([row, row], axis=1)


def tile_bias(table, first, tiles):
    return [twice(table[first + t : first + t + 1, :]) for t in range(tiles)]


def add_tiles(scores, biases):
    parts = [
        scores[t * TILE : (t + 1) * TILE, :] * SCALE2 + bias for t, bias in enumerate(biases)
    ]
    return parts[0] if len(parts) == 1 else jnp.concatenate(parts, axis=0)


def tail_bias(row_list):
    rows = row_list.shape[1]
    cut = jnp.sum((row_list == 0).astype(jnp.int32), axis=1, keepdims=True)
    key_at = lax.broadcasted_iota(jnp.int32, (rows, rows), 0)
    row_at = lax.broadcasted_iota(jnp.int32, (rows, rows), 1)
    allowed = ((key_at < cut) == (row_at < cut)) & (key_at <= row_at)
    return twice(jnp.where(allowed, 0.0, NEG).astype(F32))


def is_odd():
    return lax.rem(lax.axis_index("dp"), 2) == 1


def value_part_late():
    return jnp.logical_and(jnp.logical_not(is_odd()), lax.axis_index("ctx") > 0)


def load_copies(ins, q_ref, g_ref, k_ref, v_ref, small_refs, sems):
    q_in, g_in, tk_in, tv_in, ok_in, ov_in, *small_ins = ins
    tail = tk_in.shape[0]
    moves = list(zip(small_ins, small_refs)) + [
        (tk_in, k_ref.at[:tail]), (ok_in, k_ref.at[tail:]), (q_in, q_ref),
        (tv_in, v_ref.at[:tail]), (ov_in, v_ref.at[tail:]), (g_in, g_ref),
    ]
    copies = [pltpu.make_async_copy(a, b, sems.at[i]) for i, (a, b) in enumerate(moves)]
    for copy in copies:
        copy.start()
    return copies


def near_key_work(
    ctx, own, copies, q_ref, k_ref, p_ref, stats_ref, table_ref, rl_ref, ro_ref, rt_ref, rs_ref, rc_ref
):
    heads = k_ref.shape[1] // WIDTH
    per_head = q_ref.shape[1] // PAIR // heads
    reads = ro_ref.shape[1]
    slots = table_ref.shape[0]
    for copy in copies[:4]:
        copy.wait()
    row_list = rl_ref[...]
    owner = ro_ref[...] - lax.axis_index("ctx")
    owner = jnp.where(owner < 0, owner + ctx, owner)
    wanted = owner * own + rt_ref[...]
    live = lax.broadcasted_iota(jnp.int32, (1, reads), 1) < rc_ref[0]
    wanted = jnp.where(live, wanted, -1)
    hit = lax.broadcasted_iota(jnp.int32, (slots, reads), 0) == wanted
    first = rs_ref[...] == 0
    count0 = jnp.sum(jnp.where(hit & first, 1.0, 0.0), axis=1, keepdims=True)
    count1 = jnp.sum(jnp.where(hit & jnp.logical_not(first), 1.0, 0.0), axis=1, keepdims=True)
    count = jnp.where(row_list == 0, count0, count1)
    table = jnp.where(count > 0.5, jnp.log2(jnp.maximum(count, 1.0)), NEG)
    table_ref[...] = table
    biases = [tail_bias(row_list)] + tile_bias(table, 0, own)
    for copy in copies[4:7]:
        copy.wait()
    for head in range(heads):
        cols = slice(head * WIDTH, (head + 1) * WIDTH)
        for i in range(per_head):
            pair = head * per_head + i
            at = columns(pair, PAIR)
            s = add_tiles(dot_nt(k_ref[:, cols], pair_rows(q_ref, pair)), biases)
            top = jnp.max(s, axis=0, keepdims=True)
            p = jnp.exp2(s - top)
            p_ref[head, :, columns(i, PAIR)] = p
            stats_ref[0:1, at] = top
            stats_ref[1:2, at] = jnp.sum(p, axis=0, keepdims=True)


def near_value_work(g_ref, v_ref, p_ref, d_ref, stats_ref):
    heads = v_ref.shape[1] // WIDTH
    per_head = g_ref.shape[1] // PAIR // heads
    for head in range(heads):
        cols = slice(head * WIDTH, (head + 1) * WIDTH)
        for i in range(per_head):
            pair = head * per_head + i
            here = columns(i, PAIR)
            d = dot_nt(v_ref[:, cols], pair_rows(g_ref, pair))
            d_ref[head, :, here] = d
            cross = jnp.sum(p_ref[head, :, here] * d, axis=0, keepdims=True)
            stats_ref[2:3, columns(pair, PAIR)] = cross


def near_kernel(ctx, early, *refs):
    ins, rc_ref, rest = refs[:10], refs[10], refs[11 if early else 11 + NEAR_OUTS :]
    q_ref, g_ref, k_ref, v_ref, p_ref, d_ref, stats_ref, table_ref = rest[:NEAR_OUTS]
    small_refs, sems = rest[NEAR_OUTS:-1], rest[-1]
    own = ins[4].shape[0] // TILE

    def key_part():
        copies = load_copies(ins, q_ref, g_ref, k_ref, v_ref, small_refs, sems)
        near_key_work(
            ctx, own, copies, q_ref, k_ref, p_ref, stats_ref, table_ref, *small_refs, rc_ref
        )
        for copy in copies[7:]:
            copy.wait()

    if early:
        pl.when(is_odd())(key_part)
    else:
        pl.when(jnp.logical_not(is_odd()))(key_part)

        @pl.when(jnp.logical_not(value_part_late()))
        def value_part():
            near_value_work(g_ref, v_ref, p_ref, d_ref, stats_ref)


def far_key_kernel(
    unroll, q_ref, g_ref, k_ref, stats_ref, table_ref, back_ref, p_ref, fin_ref, *total_ref
):
    far_tiles = k_ref.shape[0] // TILE
    heads = k_ref.shape[1] // WIDTH
    per_head = q_ref.shape[1] // PAIR // heads
    shifts, own_keys, _ = back_ref.shape
    biases = tile_bias(table_ref[...], own_keys // TILE, far_tiles)
    for head in range(heads):
        cols = slice(head * WIDTH, (head + 1) * WIDTH)

        def step(i):
            pair = head * per_head + i
            at = columns(pair, PAIR)
            here = columns(i, PAIR)
            s = add_tiles(dot_nt(k_ref[:, cols], pair_rows(q_ref, pair)), biases)
            near_top = stats_ref[0:1, at]
            top = jnp.maximum(near_top, jnp.max(s, axis=0, keepdims=True))
            p = jnp.exp2(s - top)
            fade = jnp.exp2(near_top - top)
            inverse = 1.0 / (stats_ref[1:2, at] * fade + jnp.sum(p, axis=0, keepdims=True))
            fin_ref[0:1, at] = fade * inverse
            p = (p * inverse).astype(BF16)
            p_ref[head, :, here] = p
            return dot_nn(p, pair_rows(g_ref, pair))

        dv = added(per_head, unroll, step, total_ref).astype(BF16)
        for shift in range(shifts):
            back_ref[shift, :, cols] = dv[shift * own_keys : (shift + 1) * own_keys]


def far_value_kernel(
    unroll, q_ref, g_ref, v_ref, p_ref, fin_ref, near_v_ref, near_p_ref, *refs
):
    d_ref, stats_ref, back_ref, ds_ref, delta_ref, *total_ref = refs[2:]
    heads = v_ref.shape[1] // WIDTH
    per_head = q_ref.shape[1] // PAIR // heads
    shifts, own_keys, _ = back_ref.shape

    @pl.when(value_part_late())
    def value_part():
        near_value_work(g_ref, near_v_ref, near_p_ref, d_ref, stats_ref)

    for head in range(heads):
        cols = slice(head * WIDTH, (head + 1) * WIDTH)

        def step(i):
            pair = head * per_head + i
            at = columns(pair, PAIR)
            here = columns(i, PAIR)
            d = dot_nt(v_ref[:, cols], pair_rows(g_ref, pair))
            p = p_ref[head, :, here].astype(F32)
            delta = stats_ref[2:3, at] * fin_ref[0:1, at] + jnp.sum(p * d, axis=0, keepdims=True)
            delta_ref[0:1, at] = delta
            ds = (p * (d - delta)).astype(BF16)
            ds_ref[head, :, here] = ds
            return dot_nn(ds, pair_rows(q_ref, pair))

        dk = (added(per_head, unroll, step, total_ref) * SCALE).astype(BF16)
        for shift in range(shifts):
            back_ref[shift, :, cols] = dk[shift * own_keys : (shift + 1) * own_keys]


def sum_kernel(after_ref, own_ref, *refs):
    total = own_ref[...]
    for ref in refs[:-1]:
        total = total + ref[...].astype(F32)
    refs[-1][...] = total


def last_kernel(
    unroll, q_ref, g_ref, k_ref, p_ref, d_ref, fin_ref, delta_ref, fk_ref, fds_ref,
    dq_ref, dtk_ref, dtv_ref, dok_ref, dov_ref, low_ref, ds_ref,
):
    tail = dtk_ref.shape[0]
    heads = k_ref.shape[1] // WIDTH
    per_head = q_ref.shape[1] // PAIR // heads
    for head in range(heads):
        cols = slice(head * WIDTH, (head + 1) * WIDTH)

        def step(i):
            pair = head * per_head + i
            at = columns(pair, PAIR)
            here = columns(i, PAIR)
            p = p_ref[head, :, here] * fin_ref[0:1, at]
            ds = (p * (d_ref[head, :, here] - delta_ref[0:1, at])).astype(BF16)
            low_ref[head, :, here] = p.astype(BF16)
            ds_ref[head, :, here] = ds
            dq = dot_tn(k_ref[:, cols], ds) + dot_tn(fk_ref[:, cols], fds_ref[head, :, here])
            dq = dq * SCALE
            dq = jnp.concatenate([dq[:, :WIDTH].T, dq[:, WIDTH:].T], axis=1)
            dq_ref[:, at] = dq.astype(BF16)

        repeat(per_head, unroll, step)
        dk = dot_nn(ds_ref[head], stacked_rows(q_ref, head, 2 * per_head)) * SCALE
        dv = dot_nn(low_ref[head], stacked_rows(g_ref, head, 2 * per_head))
        dtk_ref[:, cols] = dk[:tail].astype(BF16)
        dtv_ref[:, cols] = dv[:tail].astype(BF16)
        dok_ref[:, cols] = dk[tail:]
        dov_ref[:, cols] = dv[tail:]


def call(kernel, spaces, outs, scratch, flops, mib, *args, aliases={}):
    vmem = pl.BlockSpec(memory_space=pltpu.VMEM)
    moved = sum(a.size * a.dtype.itemsize for a in args) + sum(
        math.prod(o.shape) * jnp.dtype(o.dtype).itemsize for o in outs
    )
    return pl.pallas_call(
        kernel,
        out_shape=outs,
        in_specs=[pl.BlockSpec(memory_space=space) for space in spaces],
        out_specs=[vmem] * len(outs),
        scratch_shapes=scratch,
        input_output_aliases=aliases,
        compiler_params=pltpu.CompilerParams(vmem_limit_bytes=mib * 2**20),
        cost_estimate=pl.CostEstimate(flops=flops, bytes_accessed=moved, transcendentals=0),
    )(*args)


def body(q, g, tk, tv, ck, cv, row_list, read_owner, read_tile, read_list, read_count):
    ctx = lax.axis_size("ctx")
    rows, q_width = q.shape
    kv_width = tk.shape[1]
    heads = kv_width // WIDTH
    group_rows = rows * (q_width // kv_width)
    own_keys = ck.shape[0]
    own = own_keys // TILE
    far_keys = (ctx - 1) * own_keys
    near_keys = rows + own_keys
    slots = -(-ctx * own // 8) * 8
    unroll = ctx <= 2
    row_list = row_list.reshape(1, rows)

    def shifted(x, shift):
        return lax.ppermute(x, "ctx", [(o, (o - shift) % ctx) for o in range(ctx)])

    far_k = [shifted(ck, s) for s in range(1, ctx)]
    shape = jax.ShapeDtypeStruct
    product = 2 * q_width * rows * WIDTH
    small = read_owner.shape
    here = [
        pltpu.with_memory_space_constraint(a, pltpu.HBM)
        for a in (q, g, tk, tv, ck, cv, row_list, read_owner, read_tile, read_list)
    ]
    near_outs = [
        pltpu.VMEM(q.shape, BF16),
        pltpu.VMEM(g.shape, BF16),
        pltpu.VMEM((near_keys, kv_width), BF16),
        pltpu.VMEM((near_keys, kv_width), BF16),
        pltpu.VMEM((heads, near_keys, group_rows), F32),
        pltpu.VMEM((heads, near_keys, group_rows), F32),
        pltpu.VMEM((8, heads * group_rows), F32),
        pltpu.VMEM((slots, rows), F32),
    ]
    near = [
        [pltpu.HBM] * len(here) + [pltpu.SMEM],
        near_outs,
        [
            pltpu.VMEM(row_list.shape, jnp.int32),
            pltpu.VMEM(small, jnp.int32),
            pltpu.VMEM(small, jnp.int32),
            pltpu.VMEM(small, jnp.int32),
            pltpu.SemaphoreType.DMA((10,)),
        ],
        2 * product * near_keys // WIDTH,
        32,
        *here, read_count,
    ]
    early = list(call(functools.partial(near_kernel, ctx, True), *near))
    own_v, early[-1] = lax.optimization_barrier((cv, early[-1]))
    far_v = [shifted(own_v, s) for s in range(1, ctx)]
    near[0] = near[0] + [pltpu.VMEM] * NEAR_OUTS
    first = len(here) + 1
    early = [pltpu.with_memory_space_constraint(a, pltpu.VMEM) for a in early]
    q, g, near_k, near_v, near_p, near_d, stats, table = call(
        functools.partial(near_kernel, ctx, False), *near, *early,
        aliases={first + i: i for i in range(NEAR_OUTS)},
    )
    mib = 32 if unroll else 60
    total = [] if unroll else [pltpu.VMEM((far_keys, WIDTH), F32)]
    far_k = far_k[0] if ctx == 2 else jnp.concatenate(far_k, axis=0)
    back_v, far_p, fin = call(
        functools.partial(far_key_kernel, unroll),
        [pltpu.VMEM] * 5,
        [
            shape((ctx - 1, own_keys, kv_width), BF16),
            shape((heads, far_keys, group_rows), BF16),
            shape((8, heads * group_rows), F32),
        ],
        total,
        2 * product * far_keys // WIDTH,
        mib,
        q, g, far_k, stats, table,
    )
    returned_v = [shifted(back_v[s - 1], -s) for s in range(1, ctx)]
    far_v = far_v[0] if ctx == 2 else jnp.concatenate(far_v, axis=0)
    near_d, stats = (pltpu.with_memory_space_constraint(a, pltpu.VMEM) for a in (near_d, stats))
    near_d, stats, back_k, far_ds, delta = call(
        functools.partial(far_value_kernel, unroll),
        [pltpu.VMEM] * 9,
        [
            pltpu.VMEM(near_d.shape, F32),
            pltpu.VMEM(stats.shape, F32),
            shape((ctx - 1, own_keys, kv_width), BF16),
            shape((heads, far_keys, group_rows), BF16),
            shape((8, heads * group_rows), F32),
        ],
        total,
        2 * product * far_keys // WIDTH,
        mib,
        q, g, far_v, far_p, fin, near_v, near_p, near_d, stats,
        aliases={7: 0, 8: 1},
    )
    returned_k = [shifted(back_k[s - 1], -s) for s in range(1, ctx)]
    dq, dtk, dtv, dok, dov = call(
        functools.partial(last_kernel, unroll),
        [pltpu.VMEM] * 9,
        [
            shape(q.shape, BF16),
            shape(tk.shape, BF16),
            shape(tv.shape, BF16),
            shape(ck.shape, F32),
            shape(cv.shape, F32),
        ],
        [pltpu.VMEM((heads, near_keys, group_rows), BF16)] * 2,
        product * (3 * near_keys + far_keys) // WIDTH,
        mib,
        q, g, near_k, near_p, near_d, fin, delta, far_k, far_ds,
    )

    def summed(after, own_sum, returned):
        return call(
            sum_kernel,
            [pltpu.HBM] + [pltpu.VMEM] * (1 + len(returned)),
            [shape(own_sum.shape, F32)],
            [],
            0,
            mib,
            pltpu.with_memory_space_constraint(after, pltpu.HBM), own_sum, *returned,
        )[0]

    dov = summed(dq, dov, returned_v)
    dok = summed(dov, dok, returned_k)
    return dq, dtk, dtv, dok, dov


def solution(mesh):
    wide = P(("dp", "ctx"), "tp")
    lone = P(("dp", "ctx"))
    flat = P(("dp", "ctx"), None)
    return jax.shard_map(
        body,
        mesh=mesh,
        in_specs=(wide,) * 6 + (lone, flat, flat, flat, lone),
        out_specs=(wide,) * 5,
        check_vma=False,
    )
```

profile of v0, /device:TPU:0, one launch (start us, length us, event | category | flops | bytes accessed | tf_op | source)
XLA Modules:
  0.0 18.2 jit_solution(7373301218785458142)
XLA Ops:
  0.6 3.0 %collective-permute-start.1 = (bf16[256,256]{1,0:T(8,128)(2,1)}, bf16[256,256]{1,0:T(8,128)(2,1)S(1)}, u32[]{:S(2)}, u32[]{:S(2)}) collective-permute-start(bf16[256,256]{1,0:T(8,128)(2,1)} %refs_4_.3), channel_id=1, source_target_pairs={{0,16},{16,0},{1,17},{17,1},{2,18},{18,2},{3,19},{19,3},{4,20},{20... | collective-permute-start | bytes 393224 | tf_op jit(solution)/shard_map/ppermute | solution.py:333
  4.3 0.1 shard_map.146
  4.4 0.1 collective-permute-start
  4.5 3.1 %shard_map.147 = (bf16[128,2048]{1,0:T(8,128)(2,1)S(1)}, bf16[128,2048]{1,0:T(8,128)(2,1)S(1)}, bf16[384,256]{1,0:T(8,128)(2,1)S(1)}, bf16[384,256]{1,0:T(8,128)...) custom-call(bf16[128,2048]{1,0:T(8,128)(2,1)} %refs_0_.3, ...), custom_call_target="tpu_custom_call", output_to_operand_aliasing={{0}: (11, {}), {1}: (12, {}), {2}: (13, {}), {3}: (14, {}),... | custom-call | flops 402653184 | bytes 17048356 | tf_op jit(solution)/shard_map/pallas_call | solution.py:306
  7.6 0.0 collective-permute-done.1.k_ref.fk_ref
  7.6 1.2 %shard_map.148 = (bf16[1,256,256]{2,1,0:T(8,128)(2,1)S(1)}, bf16[2,256,1024]{2,1,0:T(8,128)(2,1)S(1)}, f32[8,2048]{1,0:T(8,128)S(1)}) custom-call(bf16[128,2048]{1,0:T(8,128)(2,1)S(1)} %get-tuple-element.44.q_ref, bf16[128,2048]{1,0:T(8,128)(2,1)S(1)} %get-tuple-element.45.g_ref, bf16[256,256]{1,0:T(8,128)(2,1)S(1)} %collective-permute-done.1.k_ref.fk_ref, ...), custom_call_target="tpu_custom_call" | custom-call | flops 268435456 | bytes 2494464 | tf_op jit(solution)/shard_map/pallas_call | solution.py:306
  8.7 1.6 %collective-permute-start.2 = (bf16[256,256]{1,0:T(8,128)(2,1)S(1)}, bf16[256,256]{1,0:T(8,128)(2,1)S(1)}, u32[]{:S(2)}, u32[]{:S(2)}) collective-permute-start(bf16[256,256]{1,0:T(8,128)(2,1)S(1)} %bitcast.3), channel_id=1, source_target_pairs={{0,16},{16,0},{1,17},{17,1},{2,18},{18,2},{3,19},{19,3},{4,20},{20... | collective-permute-start | bytes 393224 | tf_op jit(solution)/shard_map/ppermute | solution.py:333
  10.3 0.0 collective-permute-done.v_ref
  10.3 1.1 %shard_map.149 = (f32[2,384,1024]{2,1,0:T(8,128)S(1)}, f32[8,2048]{1,0:T(8,128)S(1)}, bf16[1,256,256]{2,1,0:T(8,128)(2,1)S(1)}, bf16[2,256,1024]{2,1,0:T(8,128)(2,1)S(1)}, f32[8,2048]{1,0:T(8,128)S(1)}) custom-call(bf16[128,2048]{1,0:T(8,128)(2,1)S(1)} %get-tuple-element.44.q_ref, ...), custom_call_target="tpu_custom_call", output_to_operand_aliasing={{0}: (7, {}), {1}: (8, {})} | custom-call | flops 268435456 | bytes 13303808 | tf_op jit(solution)/shard_map/pallas_call | solution.py:306
  11.5 1.8 %collective-permute-start.3 = (bf16[256,256]{1,0:T(8,128)(2,1)S(1)}, bf16[256,256]{1,0:T(8,128)(2,1)S(1)}, u32[]{:S(2)}, u32[]{:S(2)}) collective-permute-start(bf16[256,256]{1,0:T(8,128)(2,1)S(1)} %bitcast.4), channel_id=1, source_target_pairs={{0,16},{16,0},{1,17},{17,1},{2,18},{18,2},{3,19},{19,3},{4,20},{20... | collective-permute-start | bytes 393224 | tf_op jit(solution)/shard_map/ppermute | solution.py:333
  13.2 2.3 %shard_map.150 = (bf16[128,2048]{1,0:T(8,128)(2,1)}, bf16[128,256]{1,0:T(8,128)(2,1)}, bf16[128,256]{1,0:T(8,128)(2,1)}, f32[256,256]{1,0:T(8,128)S(1)}, f32[256,256]{1,0:T(8,128)S(1)}) custom-call(bf16[128,2048]{1,0:T(8,128)(2,1)S(1)} %get-tuple-element.44.q_ref, bf16[128,2048]{1,0:T(8,128)(2,1)S(1)} %get-tuple-element.45.g_ref, ...), custom_call_target="tpu_custom_call" | custom-call | flops 738197504 | bytes 10027008 | tf_op jit(solution)/shard_map/pallas_call | solution.py:306
  15.5 0.0 collective-permute-done.2.refs_0_
  15.5 0.7 %shard_map.151.after_ref = f32[256,256]{1,0:T(8,128)} custom-call(bf16[128,2048]{1,0:T(8,128)(2,1)} %get-tuple-element.30.after_ref, f32[256,256]{1,0:T(8,128)S(1)} %get-tuple-element.61.own_ref, bf16[256,256]{1,0:T(8,128)(2,1)S(1)} %collective-permute-done.2.refs_0_), custom_call_target="tpu_custom_call" | custom-call | bytes 1179648 | tf_op jit(solution)/shard_map/pallas_call | solution.py:306
  16.2 1.3 %collective-permute-done.3.refs_0_ = bf16[256,256]{1,0:T(8,128)(2,1)S(1)} collective-permute-done((bf16[256,256]{1,0:T(8,128)(2,1)S(1)}, bf16[256,256]{1,0:T(8,128)(2,1)S(1)}, u32[]{:S(2)}, u32[]{:S(2)}) %collective-permute-start.3) | collective-permute-done | bytes 131104 | tf_op jit(solution)/shard_map/ppermute | solution.py:333
  17.5 0.7 %shard_map.152 = f32[256,256]{1,0:T(8,128)} custom-call(f32[256,256]{1,0:T(8,128)} %shard_map.151.after_ref, f32[256,256]{1,0:T(8,128)S(1)} %get-tuple-element.63.own_ref, bf16[256,256]{1,0:T(8,128)(2,1)S(1)} %collective-permute-done.3.refs_0_), custom_call_target="tpu_custom_call" | custom-call | bytes 917504 | tf_op jit(solution)/shard_map/pallas_call | solution.py:306
Async XLA Ops:
  0.6 6.9 %collective-permute-start.1 = (bf16[256,256]{1,0:T(8,128)(2,1)}, bf16[256,256]{1,0:T(8,128)(2,1)S(1)}, u32[]{:S(2)}, u32[]{:S(2)}) collective-permute-start(bf16[256,256]{1,0:T(8,128)(2,1)} %refs_4_.3), channel_id=1, source_target_pairs={{0,16},{16,0},{1,17},{17,1},{2,18},{18,2},{3,19},{19,3},{4,20},{20... | collective-permute-start | bytes 393224 | tf_op jit(solution)/shard_map/ppermute | solution.py:333
  4.4 5.9 %collective-permute-start = (bf16[256,256]{1,0:T(8,128)(2,1)}, bf16[256,256]{1,0:T(8,128)(2,1)S(1)}, u32[]{:S(2)}, u32[]{:S(2)}) collective-permute-start(bf16[256,256]{1,0:T(8,128)(2,1)} %refs_5_.3), channel_id=1, source_target_pairs={{0,16},{16,0},{1,17},{17,1},{2,18},{18,2},{3,19},{19,3},{4,20},{20... | collective-permute-start | bytes 393224 | tf_op jit(solution)/shard_map/ppermute | solution.py:333
  8.7 6.8 %collective-permute-start.2 = (bf16[256,256]{1,0:T(8,128)(2,1)S(1)}, bf16[256,256]{1,0:T(8,128)(2,1)S(1)}, u32[]{:S(2)}, u32[]{:S(2)}) collective-permute-start(bf16[256,256]{1,0:T(8,128)(2,1)S(1)} %bitcast.3), channel_id=1, source_target_pairs={{0,16},{16,0},{1,17},{17,1},{2,18},{18,2},{3,19},{19,3},{4,20},{20... | collective-permute-start | bytes 393224 | tf_op jit(solution)/shard_map/ppermute | solution.py:333
  11.5 6.0 %collective-permute-start.3 = (bf16[256,256]{1,0:T(8,128)(2,1)S(1)}, bf16[256,256]{1,0:T(8,128)(2,1)S(1)}, u32[]{:S(2)}, u32[]{:S(2)}) collective-permute-start(bf16[256,256]{1,0:T(8,128)(2,1)S(1)} %bitcast.4), channel_id=1, source_target_pairs={{0,16},{16,0},{1,17},{17,1},{2,18},{18,2},{3,19},{19,3},{4,20},{20... | collective-permute-start | bytes 393224 | tf_op jit(solution)/shard_map/ppermute | solution.py:333
where the time goes:
time: 18.4 us; the launch traced here: 18.2 us
  Pallas kernels  9.23 us (50%)
  starting transfers between devices  6.4 us (35%)
  between operations  1.33 us (7%)
  waiting for transfers between devices  1.26 us (7%)
    pallas_call x7, Pallas kernels, call(): pl.pallas_call(kernel, out_shape=outs, in_specs=[pl.BlockSpec(memory_spac...  9.23 us
    ppermute x4, starting transfers between devices, shifted(): return lax.ppermute(x, 'ctx', [(o, (o - shift) % ctx) for o in range(ctx)])  6.4 us
    ppermute x4, waiting for transfers between devices, shifted(): return lax.ppermute(x, 'ctx', [(o, (o - shift) % ctx) for o in range(ctx)])  1.26 us
  transfers between devices with their start and end apart: 4, of which 1 were waited for; matrix products, arithmetic and copies ran while one was open for 0% of the time, Pallas kernels for 47%

commit v1 on v0

--- a/solution.py
+++ b/solution.py
@@ -83,11 +83,21 @@
     return [twice(table[first + t : first + t + 1, :]) for t in range(tiles)]
 
 
-def add_tiles(scores, biases):
-    parts = [
-        scores[t * TILE : (t + 1) * TILE, :] * SCALE2 + bias for t, bias in enumerate(biases)
+def tile_weights(raw, biases, floor=None):
+    parts = [raw[t * TILE : (t + 1) * TILE, :] for t in range(len(biases))]
+    tops = [] if floor is None else [floor]
+    for t, bias in enumerate(biases):
+        if bias.shape[0] == 1:
+            tops.append(jnp.max(parts[t], axis=0, keepdims=True) * SCALE2 + bias)
+        else:
+            parts[t] = parts[t] * SCALE2 + bias
+            tops.append(jnp.max(parts[t], axis=0, keepdims=True))
+    top = functools.reduce(jnp.maximum, tops)
+    weights = [
+        jnp.exp2(part * SCALE2 + (bias - top) if bias.shape[0] == 1 else part - top)
+        for part, bias in zip(parts, biases)
     ]
-    return parts[0] if len(parts) == 1 else jnp.concatenate(parts, axis=0)
+    return (weights[0] if len(weights) == 1 else jnp.concatenate(weights, axis=0)), top
 
 
 def tail_bias(row_list):
@@ -150,9 +160,7 @@
         for i in range(per_head):
             pair = head * per_head + i
             at = columns(pair, PAIR)
-            s = add_tiles(dot_nt(k_ref[:, cols], pair_rows(q_ref, pair)), biases)
-            top = jnp.max(s, axis=0, keepdims=True)
-            p = jnp.exp2(s - top)
+            p, top = tile_weights(dot_nt(k_ref[:, cols], pair_rows(q_ref, pair)), biases)
             p_ref[head, :, columns(i, PAIR)] = p
             stats_ref[0:1, at] = top
             stats_ref[1:2, at] = jnp.sum(p, axis=0, keepdims=True)
@@ -211,16 +219,15 @@
             pair = head * per_head + i
             at = columns(pair, PAIR)
             here = columns(i, PAIR)
-            s = add_tiles(dot_nt(k_ref[:, cols], pair_rows(q_ref, pair)), biases)
             near_top = stats_ref[0:1, at]
-            top = jnp.maximum(near_top, jnp.max(s, axis=0, keepdims=True))
-            p = jnp.exp2(s - top)
+            raw = dot_nt(k_ref[:, cols], pair_rows(q_ref, pair))
+            p, top = tile_weights(raw, biases, near_top)
             fade = jnp.exp2(near_top - top)
             inverse = 1.0 / (stats_ref[1:2, at] * fade + jnp.sum(p, axis=0, keepdims=True))
             fin_ref[0:1, at] = fade * inverse
-            p = (p * inverse).astype(BF16)
-            p_ref[head, :, here] = p
-            return dot_nn(p, pair_rows(g_ref, pair))
+            p = p * inverse
+            p_ref[head, :, here] = p.astype(p_ref.dtype)
+            return dot_nn(p.astype(BF16), pair_rows(g_ref, pair))
 
         dv = added(per_head, unroll, step, total_ref).astype(BF16)
         for shift in range(shifts):
@@ -382,7 +389,7 @@
         [pltpu.VMEM] * 5,
         [
             shape((ctx - 1, own_keys, kv_width), BF16),
-            shape((heads, far_keys, group_rows), BF16),
+            shape((heads, far_keys, group_rows), F32 if unroll else BF16),
             shape((8, heads * group_rows), F32),
         ],
         total,

time: 18.4 us -> 18.4 us (level)
  starting transfers between devices: 6.4 us -> 6.13 us
  Pallas kernels: 9.23 us -> 9.42 us
    ppermute x4, starting transfers between devices: 6.4 us -> 6.13 us  [shifted(): return lax.ppermute(x, 'ctx', [(o, (o - shift) % ctx) for o in range(ctx)])]
    pallas_call x7, Pallas kernels: 9.23 us -> 9.42 us  [call(): pl.pallas_call(kernel, out_shape=outs, in_specs=[pl.BlockSpec(memory_spac...]
  transfers between devices with their start and end apart: 4 -> 4, of which waited for: 1 -> 1; matrix products, arithmetic and copies ran while one was open for 0% -> 0% of each run, Pallas kernels for 47% -> 48%
where the time goes in v1:
time: 18.4 us; the launch traced here: 18.2 us
  Pallas kernels  9.42 us (51%)
  starting transfers between devices  6.13 us (33%)
  waiting for transfers between devices  1.34 us (7%)
  between operations  1.33 us (7%)
    pallas_call x7, Pallas kernels, call(): pl.pallas_call(kernel, out_shape=outs, in_specs=[pl.BlockSpec(memory_spac...  9.42 us
    ppermute x4, starting transfers between devices, shifted(): return lax.ppermute(x, 'ctx', [(o, (o - shift) % ctx) for o in range(ctx)])  6.13 us
    ppermute x4, waiting for transfers between devices, shifted(): return lax.ppermute(x, 'ctx', [(o, (o - shift) % ctx) for o in range(ctx)])  1.34 us
  transfers between devices with their start and end apart: 4, of which 1 were waited for; matrix products, arithmetic and copies ran while one was open for 0% of the time, Pallas kernels for 48%

profile of v1, /device:TPU:0, one launch (start us, length us, event | category | flops | bytes accessed | tf_op | source)
XLA Modules:
  0.0 18.2 jit_solution(2245948729709820416)
XLA Ops:
  0.6 3.0 %collective-permute-start.1 = (bf16[256,256]{1,0:T(8,128)(2,1)}, bf16[256,256]{1,0:T(8,128)(2,1)S(1)}, u32[]{:S(2)}, u32[]{:S(2)}) collective-permute-start(bf16[256,256]{1,0:T(8,128)(2,1)} %refs_4_.3), channel_id=1, source_target_pairs={{0,16},{16,0},{1,17},{17,1},{2,18},{18,2},{3,19},{19,3},{4,20},{20... | collective-permute-start | bytes 393224 | tf_op jit(solution)/shard_map/ppermute | solution.py:340
  4.3 0.1 shard_map.146
  4.4 0.1 collective-permute-start
  4.5 3.2 %shard_map.147 = (bf16[128,2048]{1,0:T(8,128)(2,1)S(1)}, bf16[128,2048]{1,0:T(8,128)(2,1)S(1)}, bf16[384,256]{1,0:T(8,128)(2,1)S(1)}, bf16[384,256]{1,0:T(8,128)...) custom-call(bf16[128,2048]{1,0:T(8,128)(2,1)} %refs_0_.3, ...), custom_call_target="tpu_custom_call", output_to_operand_aliasing={{0}: (11, {}), {1}: (12, {}), {2}: (13, {}), {3}: (14, {}),... | custom-call | flops 402653184 | bytes 17048356 | tf_op jit(solution)/shard_map/pallas_call | solution.py:313
  7.7 0.0 collective-permute-done.1.k_ref.fk_ref
  7.7 1.3 %shard_map.148 = (bf16[1,256,256]{2,1,0:T(8,128)(2,1)S(1)}, f32[2,256,1024]{2,1,0:T(8,128)S(1)}, f32[8,2048]{1,0:T(8,128)S(1)}) custom-call(bf16[128,2048]{1,0:T(8,128)(2,1)S(1)} %get-tuple-element.44.q_ref, bf16[128,2048]{1,0:T(8,128)(2,1)S(1)} %get-tuple-element.45.g_ref, bf16[256,256]{1,0:T(8,128)(2,1)S(1)} %collective-permute-done.1.k_ref.fk_ref, ...), custom_call_target="tpu_custom_call" | custom-call | flops 268435456 | bytes 3543040 | tf_op jit(solution)/shard_map/pallas_call | solution.py:313
  8.9 1.5 %collective-permute-start.2 = (bf16[256,256]{1,0:T(8,128)(2,1)S(1)}, bf16[256,256]{1,0:T(8,128)(2,1)S(1)}, u32[]{:S(2)}, u32[]{:S(2)}) collective-permute-start(bf16[256,256]{1,0:T(8,128)(2,1)S(1)} %bitcast.3), channel_id=1, source_target_pairs={{0,16},{16,0},{1,17},{17,1},{2,18},{18,2},{3,19},{19,3},{4,20},{20... | collective-permute-start | bytes 393224 | tf_op jit(solution)/shard_map/ppermute | solution.py:340
  10.4 0.0 collective-permute-done.v_ref
  10.4 1.1 %shard_map.149 = (f32[2,384,1024]{2,1,0:T(8,128)S(1)}, f32[8,2048]{1,0:T(8,128)S(1)}, bf16[1,256,256]{2,1,0:T(8,128)(2,1)S(1)}, bf16[2,256,1024]{2,1,0:T(8,128)(2,1)S(1)}, f32[8,2048]{1,0:T(8,128)S(1)}) custom-call(bf16[128,2048]{1,0:T(8,128)(2,1)S(1)} %get-tuple-element.44.q_ref, ...), custom_call_target="tpu_custom_call", output_to_operand_aliasing={{0}: (7, {}), {1}: (8, {})} | custom-call | flops 268435456 | bytes 14352384 | tf_op jit(solution)/shard_map/pallas_call | solution.py:313
  11.6 1.6 %collective-permute-start.3 = (bf16[256,256]{1,0:T(8,128)(2,1)S(1)}, bf16[256,256]{1,0:T(8,128)(2,1)S(1)}, u32[]{:S(2)}, u32[]{:S(2)}) collective-permute-start(bf16[256,256]{1,0:T(8,128)(2,1)S(1)} %bitcast.4), channel_id=1, source_target_pairs={{0,16},{16,0},{1,17},{17,1},{2,18},{18,2},{3,19},{19,3},{4,20},{20... | collective-permute-start | bytes 393224 | tf_op jit(solution)/shard_map/ppermute | solution.py:340
  13.1 2.3 %shard_map.150 = (bf16[128,2048]{1,0:T(8,128)(2,1)}, bf16[128,256]{1,0:T(8,128)(2,1)}, bf16[128,256]{1,0:T(8,128)(2,1)}, f32[256,256]{1,0:T(8,128)S(1)}, f32[256,256]{1,0:T(8,128)S(1)}) custom-call(bf16[128,2048]{1,0:T(8,128)(2,1)S(1)} %get-tuple-element.44.q_ref, bf16[128,2048]{1,0:T(8,128)(2,1)S(1)} %get-tuple-element.45.g_ref, ...), custom_call_target="tpu_custom_call" | custom-call | flops 738197504 | bytes 10027008 | tf_op jit(solution)/shard_map/pallas_call | solution.py:313
  15.4 0.0 collective-permute-done.2.refs_0_
  15.4 0.7 %shard_map.151.after_ref = f32[256,256]{1,0:T(8,128)} custom-call(bf16[128,2048]{1,0:T(8,128)(2,1)} %get-tuple-element.30.after_ref, f32[256,256]{1,0:T(8,128)S(1)} %get-tuple-element.61.own_ref, bf16[256,256]{1,0:T(8,128)(2,1)S(1)} %collective-permute-done.2.refs_0_), custom_call_target="tpu_custom_call" | custom-call | bytes 1179648 | tf_op jit(solution)/shard_map/pallas_call | solution.py:313
  16.2 1.3 %collective-permute-done.3.refs_0_ = bf16[256,256]{1,0:T(8,128)(2,1)S(1)} collective-permute-done((bf16[256,256]{1,0:T(8,128)(2,1)S(1)}, bf16[256,256]{1,0:T(8,128)(2,1)S(1)}, u32[]{:S(2)}, u32[]{:S(2)}) %collective-permute-start.3) | collective-permute-done | bytes 131104 | tf_op jit(solution)/shard_map/ppermute | solution.py:340
  17.5 0.7 %shard_map.152 = f32[256,256]{1,0:T(8,128)} custom-call(f32[256,256]{1,0:T(8,128)} %shard_map.151.after_ref, f32[256,256]{1,0:T(8,128)S(1)} %get-tuple-element.63.own_ref, bf16[256,256]{1,0:T(8,128)(2,1)S(1)} %collective-permute-done.3.refs_0_), custom_call_target="tpu_custom_call" | custom-call | bytes 917504 | tf_op jit(solution)/shard_map/pallas_call | solution.py:313
Async XLA Ops:
  0.6 7.0 %collective-permute-start.1 = (bf16[256,256]{1,0:T(8,128)(2,1)}, bf16[256,256]{1,0:T(8,128)(2,1)S(1)}, u32[]{:S(2)}, u32[]{:S(2)}) collective-permute-start(bf16[256,256]{1,0:T(8,128)(2,1)} %refs_4_.3), channel_id=1, source_target_pairs={{0,16},{16,0},{1,17},{17,1},{2,18},{18,2},{3,19},{19,3},{4,20},{20... | collective-permute-start | bytes 393224 | tf_op jit(solution)/shard_map/ppermute | solution.py:340
  4.4 6.0 %collective-permute-start = (bf16[256,256]{1,0:T(8,128)(2,1)}, bf16[256,256]{1,0:T(8,128)(2,1)S(1)}, u32[]{:S(2)}, u32[]{:S(2)}) collective-permute-start(bf16[256,256]{1,0:T(8,128)(2,1)} %refs_5_.3), channel_id=1, source_target_pairs={{0,16},{16,0},{1,17},{17,1},{2,18},{18,2},{3,19},{19,3},{4,20},{20... | collective-permute-start | bytes 393224 | tf_op jit(solution)/shard_map/ppermute | solution.py:340
  8.9 6.5 %collective-permute-start.2 = (bf16[256,256]{1,0:T(8,128)(2,1)S(1)}, bf16[256,256]{1,0:T(8,128)(2,1)S(1)}, u32[]{:S(2)}, u32[]{:S(2)}) collective-permute-start(bf16[256,256]{1,0:T(8,128)(2,1)S(1)} %bitcast.3), channel_id=1, source_target_pairs={{0,16},{16,0},{1,17},{17,1},{2,18},{18,2},{3,19},{19,3},{4,20},{20... | collective-permute-start | bytes 393224 | tf_op jit(solution)/shard_map/ppermute | solution.py:340
  11.6 5.9 %collective-permute-start.3 = (bf16[256,256]{1,0:T(8,128)(2,1)S(1)}, bf16[256,256]{1,0:T(8,128)(2,1)S(1)}, u32[]{:S(2)}, u32[]{:S(2)}) collective-permute-start(bf16[256,256]{1,0:T(8,128)(2,1)S(1)} %bitcast.4), channel_id=1, source_target_pairs={{0,16},{16,0},{1,17},{17,1},{2,18},{18,2},{3,19},{19,3},{4,20},{20... | collective-permute-start | bytes 393224 | tf_op jit(solution)/shard_map/ppermute | solution.py:340

commit v2 on v0

--- a/solution.py
+++ b/solution.py
@@ -230,7 +230,7 @@
 def far_value_kernel(
     unroll, q_ref, g_ref, v_ref, p_ref, fin_ref, near_v_ref, near_p_ref, *refs
 ):
-    d_ref, stats_ref, back_ref, ds_ref, delta_ref, *total_ref = refs[2:]
+    d_ref, stats_ref, back_ref, ds_ref, delta_ref, terms_ref, low_ref, *total_ref = refs[2:]
     heads = v_ref.shape[1] // WIDTH
     per_head = q_ref.shape[1] // PAIR // heads
     shifts, own_keys, _ = back_ref.shape
@@ -258,6 +258,19 @@
         for shift in range(shifts):
             back_ref[shift, :, cols] = dk[shift * own_keys : (shift + 1) * own_keys]
 
+    @pl.when(is_odd())
+    def near_terms():
+        for head in range(heads):
+
+            def fill(i):
+                here = columns(i, PAIR)
+                p = near_p_ref[head, :, here] * fin_ref[0:1, columns(head * per_head + i, PAIR)]
+                low_ref[head, :, here] = p.astype(BF16)
+
+            repeat(per_head, unroll, fill)
+            rows = stacked_rows(g_ref, head, 2 * per_head)
+            terms_ref[:, head * WIDTH : (head + 1) * WIDTH] = dot_nn(low_ref[head], rows)
+
 
 def sum_kernel(after_ref, own_ref, *refs):
     total = own_ref[...]
@@ -266,8 +279,18 @@
     refs[-1][...] = total
 
 
-def last_kernel(
-    unroll, q_ref, g_ref, k_ref, p_ref, d_ref, fin_ref, delta_ref, fk_ref, fds_ref,
+def last_kernel(unroll, *refs):
+    @pl.when(jnp.logical_not(is_odd()))
+    def all_terms():
+        last_work(unroll, False, *refs)
+
+    @pl.when(is_odd())
+    def other_terms():
+        last_work(unroll, True, *refs)
+
+
+def last_work(
+    unroll, made, q_ref, g_ref, k_ref, p_ref, d_ref, fin_ref, delta_ref, fk_ref, fds_ref, terms_ref,
     dq_ref, dtk_ref, dtv_ref, dok_ref, dov_ref, low_ref, ds_ref,
 ):
     tail = dtk_ref.shape[0]
@@ -282,7 +305,8 @@
             here = columns(i, PAIR)
             p = p_ref[head, :, here] * fin_ref[0:1, at]
             ds = (p * (d_ref[head, :, here] - delta_ref[0:1, at])).astype(BF16)
-            low_ref[head, :, here] = p.astype(BF16)
+            if not made:
+                low_ref[head, :, here] = p.astype(BF16)
             ds_ref[head, :, here] = ds
             dq = dot_tn(k_ref[:, cols], ds) + dot_tn(fk_ref[:, cols], fds_ref[head, :, here])
             dq = dq * SCALE
@@ -291,7 +315,10 @@
 
         repeat(per_head, unroll, step)
         dk = dot_nn(ds_ref[head], stacked_rows(q_ref, head, 2 * per_head)) * SCALE
-        dv = dot_nn(low_ref[head], stacked_rows(g_ref, head, 2 * per_head))
+        if made:
+            dv = terms_ref[:, cols]
+        else:
+            dv = dot_nn(low_ref[head], stacked_rows(g_ref, head, 2 * per_head))
         dtk_ref[:, cols] = dk[:tail].astype(BF16)
         dtv_ref[:, cols] = dv[:tail].astype(BF16)
         dok_ref[:, cols] = dk[tail:]
@@ -393,7 +420,7 @@
     returned_v = [shifted(back_v[s - 1], -s) for s in range(1, ctx)]
     far_v = far_v[0] if ctx == 2 else jnp.concatenate(far_v, axis=0)
     near_d, stats = (pltpu.with_memory_space_constraint(a, pltpu.VMEM) for a in (near_d, stats))
-    near_d, stats, back_k, far_ds, delta = call(
+    near_d, stats, back_k, far_ds, delta, terms = call(
         functools.partial(far_value_kernel, unroll),
         [pltpu.VMEM] * 9,
         [
@@ -402,8 +429,9 @@
             shape((ctx - 1, own_keys, kv_width), BF16),
             shape((heads, far_keys, group_rows), BF16),
             shape((8, heads * group_rows), F32),
+            shape((near_keys, kv_width), F32),
         ],
-        total,
+        [pltpu.VMEM((heads, near_keys, group_rows), BF16)] + total,
         2 * product * far_keys // WIDTH,
         mib,
         q, g, far_v, far_p, fin, near_v, near_p, near_d, stats,
@@ -412,7 +440,7 @@
     returned_k = [shifted(back_k[s - 1], -s) for s in range(1, ctx)]
     dq, dtk, dtv, dok, dov = call(
         functools.partial(last_kernel, unroll),
-        [pltpu.VMEM] * 9,
+        [pltpu.VMEM] * 10,
         [
             shape(q.shape, BF16),
             shape(tk.shape, BF16),
@@ -423,7 +451,7 @@
         [pltpu.VMEM((heads, near_keys, group_rows), BF16)] * 2,
         product * (3 * near_keys + far_keys) // WIDTH,
         mib,
-        q, g, near_k, near_p, near_d, fin, delta, far_k, far_ds,
+        q, g, near_k, near_p, near_d, fin, delta, far_k, far_ds, terms,
     )
 
     def summed(after, own_sum, returned):

time: 18.4 us -> 18.6 us (1.011)
  no operation moved by 1% of the time
where the time goes in v2:
time: 18.6 us; the launch traced here: 18.5 us
  Pallas kernels  9.36 us (50%)
  starting transfers between devices  6.4 us (34%)
  waiting for transfers between devices  1.39 us (7%)
  between operations  1.33 us (7%)
    pallas_call x7, Pallas kernels, call(): pl.pallas_call(kernel, out_shape=outs, in_specs=[pl.BlockSpec(memory_spac...  9.36 us
    ppermute x4, starting transfers between devices, shifted(): return lax.ppermute(x, 'ctx', [(o, (o - shift) % ctx) for o in range(ctx)])  6.4 us
    ppermute x4, waiting for transfers between devices, shifted(): return lax.ppermute(x, 'ctx', [(o, (o - shift) % ctx) for o in range(ctx)])  1.39 us
  transfers between devices with their start and end apart: 4, of which 1 were waited for; matrix products, arithmetic and copies ran while one was open for 0% of the time, Pallas kernels for 47%

profile of v2, /device:TPU:0, one launch (start us, length us, event | category | flops | bytes accessed | tf_op | source)
XLA Modules:
  0.0 18.5 jit_solution(15316930344149011549)
XLA Ops:
  0.6 3.0 %collective-permute-start.1 = (bf16[256,256]{1,0:T(8,128)(2,1)}, bf16[256,256]{1,0:T(8,128)(2,1)S(1)}, u32[]{:S(2)}, u32[]{:S(2)}) collective-permute-start(bf16[256,256]{1,0:T(8,128)(2,1)} %refs_4_.3), channel_id=1, source_target_pairs={{0,16},{16,0},{1,17},{17,1},{2,18},{18,2},{3,19},{19,3},{4,20},{20... | collective-permute-start | bytes 393224 | tf_op jit(solution)/shard_map/ppermute | solution.py:360
  4.3 0.1 shard_map.146
  4.4 0.1 collective-permute-start
  4.5 3.1 %shard_map.147 = (bf16[128,2048]{1,0:T(8,128)(2,1)S(1)}, bf16[128,2048]{1,0:T(8,128)(2,1)S(1)}, bf16[384,256]{1,0:T(8,128)(2,1)S(1)}, bf16[384,256]{1,0:T(8,128)...) custom-call(bf16[128,2048]{1,0:T(8,128)(2,1)} %refs_0_.3, ...), custom_call_target="tpu_custom_call", output_to_operand_aliasing={{0}: (11, {}), {1}: (12, {}), {2}: (13, {}), {3}: (14, {}),... | custom-call | flops 402653184 | bytes 17048356 | tf_op jit(solution)/shard_map/pallas_call | solution.py:333
  7.6 0.0 collective-permute-done.1.k_ref.refs_7_
  7.6 1.2 %shard_map.148 = (bf16[1,256,256]{2,1,0:T(8,128)(2,1)S(1)}, bf16[2,256,1024]{2,1,0:T(8,128)(2,1)S(1)}, f32[8,2048]{1,0:T(8,128)S(1)}) custom-call(bf16[128,2048]{1,0:T(8,128)(2,1)S(1)} %get-tuple-element.45.q_ref.refs_0_, bf16[128,2048]{1,0:T(8,128)(2,1)S(1)} %get-tuple-element.46.g_ref.refs_1_, bf16[256,256]{1,0:T(8,128)(2,1)S(1)} %collective-permute-done.1.k_ref.refs_7_, ...), custom_call_target="tpu_custom_call" | custom-call | flops 268435456 | bytes 2494464 | tf_op jit(solution)/shard_map/pallas_call | solution.py:333
  8.7 1.6 %collective-permute-start.2 = (bf16[256,256]{1,0:T(8,128)(2,1)S(1)}, bf16[256,256]{1,0:T(8,128)(2,1)S(1)}, u32[]{:S(2)}, u32[]{:S(2)}) collective-permute-start(bf16[256,256]{1,0:T(8,128)(2,1)S(1)} %bitcast.3), channel_id=1, source_target_pairs={{0,16},{16,0},{1,17},{17,1},{2,18},{18,2},{3,19},{19,3},{4,20},{20... | collective-permute-start | bytes 393224 | tf_op jit(solution)/shard_map/ppermute | solution.py:360
  10.3 0.0 collective-permute-done.v_ref
  10.3 1.1 %shard_map.149 = (f32[2,384,1024]{2,1,0:T(8,128)S(1)}, f32[8,2048]{1,0:T(8,128)S(1)}, bf16[1,256,256]{2,1,0:T(8,128)(2,1)S(1)}, bf16[2,256,1024]{2,1,0:T(8,128)(...) custom-call(bf16[128,2048]{1,0:T(8,128)(2,1)S(1)} %get-tuple-element.45.q_r, ...), custom_call_target="tpu_custom_call", output_to_operand_aliasing={{0}: (7, {}), {1}: (8, {})} | custom-call | flops 268435456 | bytes 13697024 | tf_op jit(solution)/shard_map/pallas_call | solution.py:333
  11.5 1.8 %collective-permute-start.3 = (bf16[256,256]{1,0:T(8,128)(2,1)S(1)}, bf16[256,256]{1,0:T(8,128)(2,1)S(1)}, u32[]{:S(2)}, u32[]{:S(2)}) collective-permute-start(bf16[256,256]{1,0:T(8,128)(2,1)S(1)} %bitcast.4), channel_id=1, source_target_pairs={{0,16},{16,0},{1,17},{17,1},{2,18},{18,2},{3,19},{19,3},{4,20},{20... | collective-permute-start | bytes 393224 | tf_op jit(solution)/shard_map/ppermute | solution.py:360
  13.2 2.4 %shard_map.150 = (bf16[128,2048]{1,0:T(8,128)(2,1)}, bf16[128,256]{1,0:T(8,128)(2,1)}, bf16[128,256]{1,0:T(8,128)(2,1)}, f32[256,256]{1,0:T(8,128)S(1)}, f32[256,256]{1,0:T(8,128)S(1)}) custom-call(bf16[128,2048]{1,0:T(8,128)(2,1)S(1)} %get-tuple-element.45.q_ref.refs_0_, bf16[128,2048]{1,0:T(8,128)(2,1)S(1)} %get-tuple-element.46.g_ref.refs_1_, ...), custom_call_target="tpu_custom_call" | custom-call | flops 738197504 | bytes 10420224 | tf_op jit(solution)/shard_map/pallas_call | solution.py:333
  15.6 0.0 collective-permute-done.2.refs_0_
  15.6 0.7 %shard_map.151.after_ref = f32[256,256]{1,0:T(8,128)} custom-call(bf16[128,2048]{1,0:T(8,128)(2,1)} %get-tuple-element.31.after_ref, f32[256,256]{1,0:T(8,128)S(1)} %get-tuple-element.63.own_ref, bf16[256,256]{1,0:T(8,128)(2,1)S(1)} %collective-permute-done.2.refs_0_), custom_call_target="tpu_custom_call" | custom-call | bytes 1179648 | tf_op jit(solution)/shard_map/pallas_call | solution.py:333
  16.4 1.4 %collective-permute-done.3.refs_0_ = bf16[256,256]{1,0:T(8,128)(2,1)S(1)} collective-permute-done((bf16[256,256]{1,0:T(8,128)(2,1)S(1)}, bf16[256,256]{1,0:T(8,128)(2,1)S(1)}, u32[]{:S(2)}, u32[]{:S(2)}) %collective-permute-start.3) | collective-permute-done | bytes 131104 | tf_op jit(solution)/shard_map/ppermute | solution.py:360
  17.8 0.7 %shard_map.152 = f32[256,256]{1,0:T(8,128)} custom-call(f32[256,256]{1,0:T(8,128)} %shard_map.151.after_ref, f32[256,256]{1,0:T(8,128)S(1)} %get-tuple-element.65.own_ref, bf16[256,256]{1,0:T(8,128)(2,1)S(1)} %collective-permute-done.3.refs_0_), custom_call_target="tpu_custom_call" | custom-call | bytes 917504 | tf_op jit(solution)/shard_map/pallas_call | solution.py:333
Async XLA Ops:
  0.6 6.9 %collective-permute-start.1 = (bf16[256,256]{1,0:T(8,128)(2,1)}, bf16[256,256]{1,0:T(8,128)(2,1)S(1)}, u32[]{:S(2)}, u32[]{:S(2)}) collective-permute-start(bf16[256,256]{1,0:T(8,128)(2,1)} %refs_4_.3), channel_id=1, source_target_pairs={{0,16},{16,0},{1,17},{17,1},{2,18},{18,2},{3,19},{19,3},{4,20},{20... | collective-permute-start | bytes 393224 | tf_op jit(solution)/shard_map/ppermute | solution.py:360
  4.4 5.9 %collective-permute-start = (bf16[256,256]{1,0:T(8,128)(2,1)}, bf16[256,256]{1,0:T(8,128)(2,1)S(1)}, u32[]{:S(2)}, u32[]{:S(2)}) collective-permute-start(bf16[256,256]{1,0:T(8,128)(2,1)} %refs_5_.3), channel_id=1, source_target_pairs={{0,16},{16,0},{1,17},{17,1},{2,18},{18,2},{3,19},{19,3},{4,20},{20... | collective-permute-start | bytes 393224 | tf_op jit(solution)/shard_map/ppermute | solution.py:360
  8.7 6.9 %collective-permute-start.2 = (bf16[256,256]{1,0:T(8,128)(2,1)S(1)}, bf16[256,256]{1,0:T(8,128)(2,1)S(1)}, u32[]{:S(2)}, u32[]{:S(2)}) collective-permute-start(bf16[256,256]{1,0:T(8,128)(2,1)S(1)} %bitcast.3), channel_id=1, source_target_pairs={{0,16},{16,0},{1,17},{17,1},{2,18},{18,2},{3,19},{19,3},{4,20},{20... | collective-permute-start | bytes 393224 | tf_op jit(solution)/shard_map/ppermute | solution.py:360
  11.5 6.3 %collective-permute-start.3 = (bf16[256,256]{1,0:T(8,128)(2,1)S(1)}, bf16[256,256]{1,0:T(8,128)(2,1)S(1)}, u32[]{:S(2)}, u32[]{:S(2)}) collective-permute-start(bf16[256,256]{1,0:T(8,128)(2,1)S(1)} %bitcast.4), channel_id=1, source_target_pairs={{0,16},{16,0},{1,17},{17,1},{2,18},{18,2},{3,19},{19,3},{4,20},{20... | collective-permute-start | bytes 393224 | tf_op jit(solution)/shard_map/ppermute | solution.py:360

commit v3 on v0

--- a/solution.py
+++ b/solution.py
@@ -11,7 +11,8 @@
 WIDTH = 128
 TILE = 128
 PAIR = 2 * WIDTH
-NEAR_OUTS = 8
+SUM_PARTS = 4
+NEAR_OUTS = 10
 NEG = -1e30
 SCALE = 1.0 / math.sqrt(WIDTH)
 SCALE2 = SCALE * math.log2(math.e)
@@ -121,7 +122,8 @@
 
 
 def near_key_work(
-    ctx, own, copies, q_ref, k_ref, p_ref, stats_ref, table_ref, rl_ref, ro_ref, rt_ref, rs_ref, rc_ref
+    ctx, own, copies, q_ref, k_ref, qt_ref, p_ref, stats_ref, table_ref,
+    rl_ref, ro_ref, rt_ref, rs_ref, rc_ref,
 ):
     heads = k_ref.shape[1] // WIDTH
     per_head = q_ref.shape[1] // PAIR // heads
@@ -150,7 +152,9 @@
         for i in range(per_head):
             pair = head * per_head + i
             at = columns(pair, PAIR)
-            s = add_tiles(dot_nt(k_ref[:, cols], pair_rows(q_ref, pair)), biases)
+            qt = pair_rows(q_ref, pair).T
+            qt_ref[columns(pair, WIDTH), :] = qt
+            s = add_tiles(dot_nn(k_ref[:, cols], qt), biases)
             top = jnp.max(s, axis=0, keepdims=True)
             p = jnp.exp2(s - top)
             p_ref[head, :, columns(i, PAIR)] = p
@@ -158,7 +162,7 @@
             stats_ref[1:2, at] = jnp.sum(p, axis=0, keepdims=True)
 
 
-def near_value_work(g_ref, v_ref, p_ref, d_ref, stats_ref):
+def near_value_work(g_ref, v_ref, gt_ref, p_ref, d_ref, stats_ref):
     heads = v_ref.shape[1] // WIDTH
     per_head = g_ref.shape[1] // PAIR // heads
     for head in range(heads):
@@ -166,7 +170,9 @@
         for i in range(per_head):
             pair = head * per_head + i
             here = columns(i, PAIR)
-            d = dot_nt(v_ref[:, cols], pair_rows(g_ref, pair))
+            gt = pair_rows(g_ref, pair).T
+            gt_ref[columns(pair, WIDTH), :] = gt
+            d = dot_nn(v_ref[:, cols], gt)
             d_ref[head, :, here] = d
             cross = jnp.sum(p_ref[head, :, here] * d, axis=0, keepdims=True)
             stats_ref[2:3, columns(pair, PAIR)] = cross
@@ -174,14 +180,14 @@
 
 def near_kernel(ctx, early, *refs):
     ins, rc_ref, rest = refs[:10], refs[10], refs[11 if early else 11 + NEAR_OUTS :]
-    q_ref, g_ref, k_ref, v_ref, p_ref, d_ref, stats_ref, table_ref = rest[:NEAR_OUTS]
+    q_ref, g_ref, k_ref, v_ref, qt_ref, gt_ref, p_ref, d_ref, stats_ref, table_ref = rest[:NEAR_OUTS]
     small_refs, sems = rest[NEAR_OUTS:-1], rest[-1]
     own = ins[4].shape[0] // TILE
 
     def key_part():
         copies = load_copies(ins, q_ref, g_ref, k_ref, v_ref, small_refs, sems)
         near_key_work(
-            ctx, own, copies, q_ref, k_ref, p_ref, stats_ref, table_ref, *small_refs, rc_ref
+            ctx, own, copies, q_ref, k_ref, qt_ref, p_ref, stats_ref, table_ref, *small_refs, rc_ref
         )
         for copy in copies[7:]:
             copy.wait()
@@ -193,15 +199,15 @@
 
         @pl.when(jnp.logical_not(value_part_late()))
         def value_part():
-            near_value_work(g_ref, v_ref, p_ref, d_ref, stats_ref)
+            near_value_work(g_ref, v_ref, gt_ref, p_ref, d_ref, stats_ref)
 
 
 def far_key_kernel(
-    unroll, q_ref, g_ref, k_ref, stats_ref, table_ref, back_ref, p_ref, fin_ref, *total_ref
+    unroll, qt_ref, g_ref, k_ref, stats_ref, table_ref, back_ref, p_ref, fin_ref, *total_ref
 ):
     far_tiles = k_ref.shape[0] // TILE
     heads = k_ref.shape[1] // WIDTH
-    per_head = q_ref.shape[1] // PAIR // heads
+    per_head = g_ref.shape[1] // PAIR // heads
     shifts, own_keys, _ = back_ref.shape
     biases = tile_bias(table_ref[...], own_keys // TILE, far_tiles)
     for head in range(heads):
@@ -211,7 +217,7 @@
             pair = head * per_head + i
             at = columns(pair, PAIR)
             here = columns(i, PAIR)
-            s = add_tiles(dot_nt(k_ref[:, cols], pair_rows(q_ref, pair)), biases)
+            s = add_tiles(dot_nn(k_ref[:, cols], qt_ref[columns(pair, WIDTH), :]), biases)
             near_top = stats_ref[0:1, at]
             top = jnp.maximum(near_top, jnp.max(s, axis=0, keepdims=True))
             p = jnp.exp2(s - top)
@@ -230,14 +236,14 @@
 def far_value_kernel(
     unroll, q_ref, g_ref, v_ref, p_ref, fin_ref, near_v_ref, near_p_ref, *refs
 ):
-    d_ref, stats_ref, back_ref, ds_ref, delta_ref, *total_ref = refs[2:]
+    gt_ref, d_ref, stats_ref, back_ref, ds_ref, delta_ref, *total_ref = refs[3:]
     heads = v_ref.shape[1] // WIDTH
     per_head = q_ref.shape[1] // PAIR // heads
     shifts, own_keys, _ = back_ref.shape
 
     @pl.when(value_part_late())
     def value_part():
-        near_value_work(g_ref, near_v_ref, near_p_ref, d_ref, stats_ref)
+        near_value_work(g_ref, near_v_ref, gt_ref, near_p_ref, d_ref, stats_ref)
 
     for head in range(heads):
         cols = slice(head * WIDTH, (head + 1) * WIDTH)
@@ -246,7 +252,7 @@
             pair = head * per_head + i
             at = columns(pair, PAIR)
             here = columns(i, PAIR)
-            d = dot_nt(v_ref[:, cols], pair_rows(g_ref, pair))
+            d = dot_nn(v_ref[:, cols], gt_ref[columns(pair, WIDTH), :])
             p = p_ref[head, :, here].astype(F32)
             delta = stats_ref[2:3, at] * fin_ref[0:1, at] + jnp.sum(p * d, axis=0, keepdims=True)
             delta_ref[0:1, at] = delta
@@ -260,10 +266,21 @@
 
 
 def sum_kernel(after_ref, own_ref, *refs):
-    total = own_ref[...]
-    for ref in refs[:-1]:
-        total = total + ref[...].astype(F32)
-    refs[-1][...] = total
+    *terms, out_ref, total_ref, sems = refs
+    keys = own_ref.shape[0] // SUM_PARTS
+    copies = []
+    for part in range(SUM_PARTS):
+        rows = slice(part * keys, (part + 1) * keys)
+        total = own_ref[rows, :]
+        for ref in terms:
+            total = total + ref[rows, :].astype(F32)
+        total_ref[rows, :] = total
+        copies.append(
+            pltpu.make_async_copy(total_ref.at[rows], out_ref.at[rows], sems.at[part])
+        )
+        copies[-1].start()
+    for copy in copies:
+        copy.wait()
 
 
 def last_kernel(
@@ -298,8 +315,7 @@
         dov_ref[:, cols] = dv[tail:]
 
 
-def call(kernel, spaces, outs, scratch, flops, mib, *args, aliases={}):
-    vmem = pl.BlockSpec(memory_space=pltpu.VMEM)
+def call(kernel, spaces, outs, scratch, flops, mib, *args, aliases={}, out=pltpu.VMEM):
     moved = sum(a.size * a.dtype.itemsize for a in args) + sum(
         math.prod(o.shape) * jnp.dtype(o.dtype).itemsize for o in outs
     )
@@ -307,7 +323,7 @@
         kernel,
         out_shape=outs,
         in_specs=[pl.BlockSpec(memory_space=space) for space in spaces],
-        out_specs=[vmem] * len(outs),
+        out_specs=[pl.BlockSpec(memory_space=out)] * len(outs),
         scratch_shapes=scratch,
         input_output_aliases=aliases,
         compiler_params=pltpu.CompilerParams(vmem_limit_bytes=mib * 2**20),
@@ -345,6 +361,8 @@
         pltpu.VMEM(g.shape, BF16),
         pltpu.VMEM((near_keys, kv_width), BF16),
         pltpu.VMEM((near_keys, kv_width), BF16),
+        pltpu.VMEM((q_width // 2, PAIR), BF16),
+        pltpu.VMEM((q_width // 2, PAIR), BF16),
         pltpu.VMEM((heads, near_keys, group_rows), F32),
         pltpu.VMEM((heads, near_keys, group_rows), F32),
         pltpu.VMEM((8, heads * group_rows), F32),
@@ -370,7 +388,7 @@
     near[0] = near[0] + [pltpu.VMEM] * NEAR_OUTS
     first = len(here) + 1
     early = [pltpu.with_memory_space_constraint(a, pltpu.VMEM) for a in early]
-    q, g, near_k, near_v, near_p, near_d, stats, table = call(
+    q, g, near_k, near_v, qt, gt, near_p, near_d, stats, table = call(
         functools.partial(near_kernel, ctx, False), *near, *early,
         aliases={first + i: i for i in range(NEAR_OUTS)},
     )
@@ -388,15 +406,18 @@
         total,
         2 * product * far_keys // WIDTH,
         mib,
-        q, g, far_k, stats, table,
+        qt, g, far_k, stats, table,
     )
     returned_v = [shifted(back_v[s - 1], -s) for s in range(1, ctx)]
     far_v = far_v[0] if ctx == 2 else jnp.concatenate(far_v, axis=0)
-    near_d, stats = (pltpu.with_memory_space_constraint(a, pltpu.VMEM) for a in (near_d, stats))
-    near_d, stats, back_k, far_ds, delta = call(
+    gt, near_d, stats = (
+        pltpu.with_memory_space_constraint(a, pltpu.VMEM) for a in (gt, near_d, stats)
+    )
+    _, near_d, stats, back_k, far_ds, delta = call(
         functools.partial(far_value_kernel, unroll),
-        [pltpu.VMEM] * 9,
+        [pltpu.VMEM] * 10,
         [
+            pltpu.VMEM(gt.shape, BF16),
             pltpu.VMEM(near_d.shape, F32),
             pltpu.VMEM(stats.shape, F32),
             shape((ctx - 1, own_keys, kv_width), BF16),
@@ -406,8 +427,8 @@
         total,
         2 * product * far_keys // WIDTH,
         mib,
-        q, g, far_v, far_p, fin, near_v, near_p, near_d, stats,
-        aliases={7: 0, 8: 1},
+        q, g, far_v, far_p, fin, near_v, near_p, gt, near_d, stats,
+        aliases={7: 0, 8: 1, 9: 2},
     )
     returned_k = [shifted(back_k[s - 1], -s) for s in range(1, ctx)]
     dq, dtk, dtv, dok, dov = call(
@@ -430,11 +451,12 @@
         return call(
             sum_kernel,
             [pltpu.HBM] + [pltpu.VMEM] * (1 + len(returned)),
-            [shape(own_sum.shape, F32)],
-            [],
+            [pltpu.HBM(own_sum.shape, F32)],
+            [pltpu.VMEM(own_sum.shape, F32), pltpu.SemaphoreType.DMA((SUM_PARTS,))],
             0,
             mib,
             pltpu.with_memory_space_constraint(after, pltpu.HBM), own_sum, *returned,
+            out=pltpu.HBM,
         )[0]
 
     dov = summed(dq, dov, returned_v)

time: 18.4 us -> 18.4 us (level)
  Pallas kernels: 9.23 us -> 9.42 us
    pallas_call x7, Pallas kernels: 9.23 us -> 9.42 us  [call(): pl.pallas_call(kernel, out_shape=outs, in_specs=[pl.BlockSpec(memory_spac...]
  transfers between devices with their start and end apart: 4 -> 4, of which waited for: 1 -> 1; matrix products, arithmetic and copies ran while one was open for 0% -> 0% of each run, Pallas kernels for 47% -> 48%
where the time goes in v3:
time: 18.4 us; the launch traced here: 18.2 us
  Pallas kernels  9.42 us (51%)
  starting transfers between devices  6.24 us (34%)
  between operations  1.34 us (7%)
  waiting for transfers between devices  1.22 us (7%)
    pallas_call x7, Pallas kernels, call(): pl.pallas_call(kernel, out_shape=outs, in_specs=[pl.BlockSpec(memory_spac...  9.42 us
    ppermute x4, starting transfers between devices, shifted(): return lax.ppermute(x, 'ctx', [(o, (o - shift) % ctx) for o in range(ctx)])  6.24 us
    ppermute x4, waiting for transfers between devices, shifted(): return lax.ppermute(x, 'ctx', [(o, (o - shift) % ctx) for o in range(ctx)])  1.22 us
  transfers between devices with their start and end apart: 4, of which 1 were waited for; matrix products, arithmetic and copies ran while one was open for 0% of the time, Pallas kernels for 48%

profile of v3, /device:TPU:0, one launch (start us, length us, event | category | flops | bytes accessed | tf_op | source)
XLA Modules:
  0.0 18.2 jit_solution(6047162491275888751)
XLA Ops:
  0.6 3.0 %collective-permute-start.1 = (bf16[256,256]{1,0:T(8,128)(2,1)}, bf16[256,256]{1,0:T(8,128)(2,1)S(1)}, u32[]{:S(2)}, u32[]{:S(2)}) collective-permute-start(bf16[256,256]{1,0:T(8,128)(2,1)} %refs_4_.3), channel_id=1, source_target_pairs={{0,16},{16,0},{1,17},{17,1},{2,18},{18,2},{3,19},{19,3},{4,20},{20... | collective-permute-start | bytes 393224 | tf_op jit(solution)/shard_map/ppermute | solution.py:349
  4.3 0.1 shard_map.146
  4.4 0.1 collective-permute-start
  4.5 3.2 %shard_map.147 = (bf16[128,2048]{1,0:T(8,128)(2,1)S(1)}, bf16[128,2048]{1,0:T(8,128)(2,1)S(1)}, bf16[384,256]{1,0:T(8,128)(2,1)S(1)}, bf16[384,256]{1,0:T(8,128)...) custom-call(bf16[128,2048]{1,0:T(8,128)(2,1)} %refs_0_.3, ...), custom_call_target="tpu_custom_call", output_to_operand_aliasing={{0}: (11, {}), {1}: (12, {}), {2}: (13, {}), {3}: (14, {}),... | custom-call | flops 402653184 | bytes 19145508 | tf_op jit(solution)/shard_map/pallas_call | solution.py:322
  7.7 0.0 collective-permute-done.1.k_ref.fk_ref
  7.7 1.2 %shard_map.148 = (bf16[1,256,256]{2,1,0:T(8,128)(2,1)S(1)}, bf16[2,256,1024]{2,1,0:T(8,128)(2,1)S(1)}, f32[8,2048]{1,0:T(8,128)S(1)}) custom-call(bf16[1024,256]{1,0:T(8,128)(2,1)S(1)} %get-tuple-element.55.qt_ref, bf16[128,2048]{1,0:T(8,128)(2,1)S(1)} %get-tuple-element.51.g_ref, bf16[256,256]{1,0:T(8,128)(2,1)S(1)} %collective-permute-done.1.k_ref.fk_ref, ...), custom_call_target="tpu_custom_call" | custom-call | flops 268435456 | bytes 2494464 | tf_op jit(solution)/shard_map/pallas_call | solution.py:322
  8.9 1.4 %collective-permute-start.2 = (bf16[256,256]{1,0:T(8,128)(2,1)S(1)}, bf16[256,256]{1,0:T(8,128)(2,1)S(1)}, u32[]{:S(2)}, u32[]{:S(2)}) collective-permute-start(bf16[256,256]{1,0:T(8,128)(2,1)S(1)} %bitcast.3), channel_id=1, source_target_pairs={{0,16},{16,0},{1,17},{17,1},{2,18},{18,2},{3,19},{19,3},{4,20},{20... | collective-permute-start | bytes 393224 | tf_op jit(solution)/shard_map/ppermute | solution.py:349
  10.3 0.0 collective-permute-done.v_ref
  10.3 1.1 %shard_map.149 = (bf16[1024,256]{1,0:T(8,128)(2,1)S(1)}, f32[2,384,1024]{2,1,0:T(8,128)S(1)}, f32[8,2048]{1,0:T(8,128)S(1)}, bf16[1,256,256]{2,1,0:T(8,128)(2,1)...) custom-call(bf16[128,2048]{1,0:T(8,128)(2,1)S(1)} %get-tuple-element, ...), custom_call_target="tpu_custom_call", output_to_operand_aliasing={{0}: (7, {}), {1}: (8, {}), {2}: (9, {})} | custom-call | flops 268435456 | bytes 14352384 | tf_op jit(solution)/shard_map/pallas_call | solution.py:322
  11.5 1.8 %collective-permute-start.3 = (bf16[256,256]{1,0:T(8,128)(2,1)S(1)}, bf16[256,256]{1,0:T(8,128)(2,1)S(1)}, u32[]{:S(2)}, u32[]{:S(2)}) collective-permute-start(bf16[256,256]{1,0:T(8,128)(2,1)S(1)} %bitcast.4), channel_id=1, source_target_pairs={{0,16},{16,0},{1,17},{17,1},{2,18},{18,2},{3,19},{19,3},{4,20},{20... | collective-permute-start | bytes 393224 | tf_op jit(solution)/shard_map/ppermute | solution.py:349
  13.2 2.3 %shard_map.150 = (bf16[128,2048]{1,0:T(8,128)(2,1)}, bf16[128,256]{1,0:T(8,128)(2,1)}, bf16[128,256]{1,0:T(8,128)(2,1)}, f32[256,256]{1,0:T(8,128)S(1)}, f32[256,256]{1,0:T(8,128)S(1)}) custom-call(bf16[128,2048]{1,0:T(8,128)(2,1)S(1)} %get-tuple-element.50.q_ref, bf16[128,2048]{1,0:T(8,128)(2,1)S(1)} %get-tuple-element.51.g_ref, ...), custom_call_target="tpu_custom_call" | custom-call | flops 738197504 | bytes 10027008 | tf_op jit(solution)/shard_map/pallas_call | solution.py:322
  15.5 0.0 collective-permute-done.2.refs_0_
  15.5 0.7 %shard_map.151.after_ref = f32[256,256]{1,0:T(8,128)} custom-call(bf16[128,2048]{1,0:T(8,128)(2,1)} %get-tuple-element.34.after_ref, f32[256,256]{1,0:T(8,128)S(1)} %get-tuple-element.69.own_ref, bf16[256,256]{1,0:T(8,128)(2,1)S(1)} %collective-permute-done.2.refs_0_), custom_call_target="tpu_custom_call" | custom-call | bytes 1179648 | tf_op jit(solution)/shard_map/pallas_call | solution.py:322
  16.3 1.2 %collective-permute-done.3.refs_0_ = bf16[256,256]{1,0:T(8,128)(2,1)S(1)} collective-permute-done((bf16[256,256]{1,0:T(8,128)(2,1)S(1)}, bf16[256,256]{1,0:T(8,128)(2,1)S(1)}, u32[]{:S(2)}, u32[]{:S(2)}) %collective-permute-start.3) | collective-permute-done | bytes 131104 | tf_op jit(solution)/shard_map/ppermute | solution.py:349
  17.5 0.7 %shard_map.152 = f32[256,256]{1,0:T(8,128)} custom-call(f32[256,256]{1,0:T(8,128)} %shard_map.151.after_ref, f32[256,256]{1,0:T(8,128)S(1)} %get-tuple-element.71.own_ref, bf16[256,256]{1,0:T(8,128)(2,1)S(1)} %collective-permute-done.3.refs_0_), custom_call_target="tpu_custom_call" | custom-call | bytes 917504 | tf_op jit(solution)/shard_map/pallas_call | solution.py:322
Async XLA Ops:
  0.6 7.1 %collective-permute-start.1 = (bf16[256,256]{1,0:T(8,128)(2,1)}, bf16[256,256]{1,0:T(8,128)(2,1)S(1)}, u32[]{:S(2)}, u32[]{:S(2)}) collective-permute-start(bf16[256,256]{1,0:T(8,128)(2,1)} %refs_4_.3), channel_id=1, source_target_pairs={{0,16},{16,0},{1,17},{17,1},{2,18},{18,2},{3,19},{19,3},{4,20},{20... | collective-permute-start | bytes 393224 | tf_op jit(solution)/shard_map/ppermute | solution.py:349
  4.4 5.9 %collective-permute-start = (bf16[256,256]{1,0:T(8,128)(2,1)}, bf16[256,256]{1,0:T(8,128)(2,1)S(1)}, u32[]{:S(2)}, u32[]{:S(2)}) collective-permute-start(bf16[256,256]{1,0:T(8,128)(2,1)} %refs_5_.3), channel_id=1, source_target_pairs={{0,16},{16,0},{1,17},{17,1},{2,18},{18,2},{3,19},{19,3},{4,20},{20... | collective-permute-start | bytes 393224 | tf_op jit(solution)/shard_map/ppermute | solution.py:349
  8.9 6.6 %collective-permute-start.2 = (bf16[256,256]{1,0:T(8,128)(2,1)S(1)}, bf16[256,256]{1,0:T(8,128)(2,1)S(1)}, u32[]{:S(2)}, u32[]{:S(2)}) collective-permute-start(bf16[256,256]{1,0:T(8,128)(2,1)S(1)} %bitcast.3), channel_id=1, source_target_pairs={{0,16},{16,0},{1,17},{17,1},{2,18},{18,2},{3,19},{19,3},{4,20},{20... | collective-permute-start | bytes 393224 | tf_op jit(solution)/shard_map/ppermute | solution.py:349
  11.5 6.0 %collective-permute-start.3 = (bf16[256,256]{1,0:T(8,128)(2,1)S(1)}, bf16[256,256]{1,0:T(8,128)(2,1)S(1)}, u32[]{:S(2)}, u32[]{:S(2)}) collective-permute-start(bf16[256,256]{1,0:T(8,128)(2,1)S(1)} %bitcast.4), channel_id=1, source_target_pairs={{0,16},{16,0},{1,17},{17,1},{2,18},{18,2},{3,19},{19,3},{4,20},{20... | collective-permute-start | bytes 393224 | tf_op jit(solution)/shard_map/ppermute | solution.py:349
